TPU v7x, 32 devices: a whole 2x2x4 slice. The times are simulated.
32 devices in a mesh: fsdp: 16 (over z, y, core), tp: 2 (over x).
Axes of the slice: x: 2, y: 2, z: 4, core: 2. Of those that a mesh axis runs over, the one named last changes fastest.
Arguments:
- hidden: bfloat16 [16384, 1024], P(('fsdp', 'tp')), may hold values from -6 to 6
- norm_gain: bfloat16 [1024], P('fsdp'), may hold values from 0.5 to 1.5
- weight_gate: bfloat16 [1024, 2048], P('fsdp', 'tp'), may hold values from -0.1875 to 0.1875
- weight_inner: bfloat16 [1024, 2048], P('fsdp', 'tp'), may hold values from -0.1875 to 0.1875
- weight_shared: bfloat16 [1024, 256], P('fsdp'), may hold values from -0.1875 to 0.1875
- weight_step: bfloat16 [1024, 32], P('fsdp', 'tp'), may hold values from -0.1875 to 0.1875
- filter_inner: bfloat16 [4, 2048], P(None, 'tp'), may hold values from -0.5 to 0.5
- bias_inner: bfloat16 [2048], P('tp'), may hold values from -0.5 to 0.5
- filter_shared: bfloat16 [4, 256], replicated, may hold values from -0.5 to 0.5
- bias_shared: bfloat16 [256], replicated, may hold values from -0.5 to 0.5
- step_bias: bfloat16 [32], P('tp'), may hold values from -8 to -4
- log_rate: bfloat16 [32], P('tp'), may hold values from -1 to 2
- skip_gain: bfloat16 [32], P('tp'), may hold values from 0.5 to 1.5
- gate_gain: bfloat16 [2048], P('tp'), may hold values from 0.5 to 1.5
- weight_out: bfloat16 [1024, 2048], P('fsdp', 'tp'), may hold values from -0.125 to 0.125
- segments: int32 [16, 1024], P('fsdp'), may hold values from 0 to 6, as said below
- cotangent: bfloat16 [16384, 1024], P(('fsdp', 'tp')), may hold values from -6 to 6
Outputs:
- layer_out: bfloat16 [16384, 1024], P(('fsdp', 'tp'))
- grad_hidden: float32 [16384, 1024], P(('fsdp', 'tp'))
- grad_norm_gain: float32 [1024], P('fsdp')
- grad_weight_gate: float32 [1024, 2048], P('fsdp', 'tp')
- grad_weight_inner: float32 [1024, 2048], P('fsdp', 'tp')
- grad_weight_shared: float32 [1024, 256], P('fsdp')
- grad_weight_step: float32 [1024, 32], P('fsdp', 'tp')
- grad_filter_inner: float32 [4, 2048], P(None, 'tp')
- grad_bias_inner: float32 [2048], P('tp')
- grad_filter_shared: float32 [4, 256], replicated
- grad_bias_shared: float32 [256], replicated
- grad_step_bias: float32 [32], P('tp')
- grad_log_rate: float32 [32], P('tp')
- grad_skip_gain: float32 [32], P('tp')
- grad_gate_gain: float32 [2048], P('tp')
- grad_weight_out: float32 [1024, 2048], P('fsdp', 'tp')
Inputs may be any that keep to these rules, and one draw needn't show every extreme that they name: `segments`: in each sequence the numbers start at 0, never fall, and rise by one where a new document begins; every document has 200 to 2000 positions, except the first and the last of a sequence, which the sequence's ends may cut.
All inputs are finite; a program needn't handle non-finite values.
Results may differ from a plain program's by a relative error of at most 0.014.
Values may be sent and summed in bfloat16 or wider, within the bound.
No kernel may reach another device: no remote copies, remote signals or barrier semaphores. Data moves between devices by JAX's collectives and lax.ppermute only.
A program may use at most 192 MiB of HBM per device.

v0:
```python
import jax
import jax.numpy as jnp
from jax import lax
from jax.sharding import PartitionSpec as P

INNER = 2048
NS = 128
BLOCK = 256


EPSILON = 1e-05
HIGH = lax.Precision.HIGHEST


def block_scan(inner_x, step_val, log_step, shared_b, shared_c, seg_line):
    length, num_heads, head_size = inner_x.shape
    nblocks = length // BLOCK

    def split(array):
        return array.reshape((nblocks, BLOCK) + array.shape[1:])

    def block_step(carried, block_in):
        state_now, last_doc = carried
        x_blk, dt_blk, la_blk, b_blk, c_blk, seg_blk = block_in
        cumulative = jnp.cumsum(la_blk, axis=0)
        order = jnp.arange(BLOCK)
        visible = (seg_blk[:, None] == seg_blk[None, :]) & (order[:, None] >= order[None, :])
        log_gap = cumulative[:, None, :] - cumulative[None, :, :]
        decays = jnp.exp(jnp.where(visible[:, :, None], log_gap, -jnp.inf))
        inner_cb = jnp.dot(c_blk, b_blk.T, precision=HIGH)
        mixing_w = inner_cb[:, :, None] * decays * dt_blk[None, :, :]
        y_block = jnp.einsum("tsh,shp->thp", mixing_w, x_blk, precision=HIGH)
        keep_state = (seg_blk == last_doc).astype(jnp.float32)
        carried_in = jnp.einsum("tn,hpn->thp", c_blk, state_now, precision=HIGH)
        y_block = y_block + carried_in * (jnp.exp(cumulative) * keep_state[:, None])[:, :, None]
        end_doc = seg_blk[BLOCK - 1]
        tail_w = (
            jnp.exp(cumulative[BLOCK - 1][None, :] - cumulative)
            * (seg_blk == end_doc).astype(jnp.float32)[:, None]
            * dt_blk
        )
        next_state = jnp.einsum("sh,shp,sn->hpn", tail_w, x_blk, b_blk, precision=HIGH)
        carry_on = jnp.exp(cumulative[BLOCK - 1]) * (last_doc == end_doc).astype(jnp.float32)
        next_state = next_state + state_now * carry_on[:, None, None]
        return ((next_state, end_doc), y_block)

    initial = (
        jnp.zeros((num_heads, head_size, shared_b.shape[1]), jnp.float32),
        jnp.array(-1, jnp.int32),
    )
    blocks_in = (
        split(inner_x),
        split(step_val),
        split(log_step),
        split(shared_b),
        split(shared_c),
        split(seg_line),
    )
    unused, y_blocks = lax.scan(jax.checkpoint(block_step), initial, blocks_in)
    return y_blocks.reshape(inner_x.shape)


def mixing(
    gate_val,
    inner_val,
    shared_val,
    step_raw,
    filters,
    biases,
    step_bias,
    log_rate,
    skip_gain,
    seg_line,
):
    length, width_in = inner_val.shape
    num_heads = step_raw.shape[1]
    head_size = width_in // num_heads
    joined = jnp.concatenate([inner_val, shared_val], axis=1)
    taps = filters.shape[0]
    conv_sum = biases[None, :] + filters[taps - 1][None, :] * joined
    for shift in range(1, taps):
        shifted = jnp.pad(joined, ((shift, 0), (0, 0)))[:length]
        prior_seg = jnp.pad(seg_line, (shift, 0), constant_values=-1)[:length]
        same_doc = (prior_seg == seg_line).astype(jnp.float32)
        conv_sum = conv_sum + filters[taps - 1 - shift][None, :] * shifted * same_doc[:, None]
    activated = jax.nn.silu(conv_sum)
    inner_x = activated[:, :width_in].reshape(length, num_heads, head_size)
    shared_b = activated[:, width_in : width_in + NS]
    shared_c = activated[:, width_in + NS :]
    step_val = jax.nn.softplus(step_raw + step_bias[None, :])
    log_step = -step_val * jnp.exp(log_rate)[None, :]
    y_heads = block_scan(inner_x, step_val, log_step, shared_b, shared_c, seg_line)
    y_heads = y_heads + skip_gain[None, :, None] * inner_x
    return y_heads.reshape(length, width_in) * jax.nn.silu(gate_val)


def transposed(grad_low, weight):
    return lax.dot_general(
        grad_low, weight, (((1,), (1,)), ((), ())), preferred_element_type=jnp.float32
    )


def weight_grad(left, right):
    return lax.dot_general(
        left, right, (((0,), (0,)), ((), ())), preferred_element_type=jnp.float32
    )


def per_device(
    hidden,
    norm_gain,
    weight_gate,
    weight_inner,
    weight_shared,
    weight_step,
    filter_inner,
    bias_inner,
    filter_shared,
    bias_shared,
    step_bias,
    log_rate,
    skip_gain,
    gate_gain,
    weight_out,
    segments,
    cotangent,
):
    gathered = (
        lax.all_gather(norm_gain, "fsdp", axis=0, tiled=True),
        lax.all_gather(weight_gate, "fsdp", axis=0, tiled=True),
        lax.all_gather(weight_inner, "fsdp", axis=0, tiled=True),
        lax.all_gather(weight_shared, "fsdp", axis=0, tiled=True),
        lax.all_gather(weight_step, "fsdp", axis=0, tiled=True),
        lax.all_gather(weight_out, "fsdp", axis=0, tiled=True),
    )
    gain_all, gate_all, inner_all, shared_all, step_all, out_all = gathered
    hidden_f = hidden.astype(jnp.float32)
    inv_rms = lax.rsqrt(jnp.mean(hidden_f * hidden_f, axis=1, keepdims=True) + EPSILON)
    x_hat = hidden_f * inv_rms
    gain_f = gain_all.astype(jnp.float32)
    normed = (x_hat * gain_f[None, :]).astype(jnp.bfloat16)
    shared_own = jnp.dot(normed, shared_all, preferred_element_type=jnp.float32).astype(
        jnp.bfloat16
    )
    normed_all, shared_seq = (
        lax.all_gather(normed, "tp", axis=0, tiled=True),
        lax.all_gather(shared_own, "tp", axis=0, tiled=True),
    )
    gate_seq = jnp.dot(normed_all, gate_all, preferred_element_type=jnp.float32).astype(
        jnp.bfloat16
    )
    inner_seq = jnp.dot(normed_all, inner_all, preferred_element_type=jnp.float32).astype(
        jnp.bfloat16
    )
    step_seq = jnp.dot(normed_all, step_all, preferred_element_type=jnp.float32).astype(
        jnp.bfloat16
    )
    seg_line = segments[0]
    filters = jnp.concatenate([filter_inner, filter_shared], axis=1).astype(jnp.float32)
    biases = jnp.concatenate([bias_inner, bias_shared], axis=0).astype(jnp.float32)

    def local_mix(
        gate_val, inner_val, shared_val, step_raw, filter_all, bias_all, offsets, rates, skips
    ):
        return mixing(
            gate_val,
            inner_val,
            shared_val,
            step_raw,
            filter_all,
            bias_all,
            offsets,
            rates,
            skips,
            seg_line,
        )

    mixed, pullback = jax.vjp(
        local_mix,
        gate_seq.astype(jnp.float32),
        inner_seq.astype(jnp.float32),
        shared_seq.astype(jnp.float32),
        step_seq.astype(jnp.float32),
        filters,
        biases,
        step_bias.astype(jnp.float32),
        log_rate.astype(jnp.float32),
        skip_gain.astype(jnp.float32),
    )
    square_sum = lax.psum(jnp.sum(mixed * mixed, axis=1), "tp")
    inv_gate = lax.rsqrt(square_sum / INNER + EPSILON)[:, None]
    gain_gate = gate_gain.astype(jnp.float32)[None, :]
    gated = (mixed * inv_gate * gain_gate).astype(jnp.bfloat16)
    out_own = lax.psum_scatter(transposed(gated, out_all), "tp", scatter_dimension=0, tiled=True)
    layer_out = (hidden_f + out_own).astype(jnp.bfloat16)
    regathered = (
        lax.all_gather(norm_gain, "fsdp", axis=0, tiled=True),
        lax.all_gather(weight_gate, "fsdp", axis=0, tiled=True),
        lax.all_gather(weight_inner, "fsdp", axis=0, tiled=True),
        lax.all_gather(weight_shared, "fsdp", axis=0, tiled=True),
        lax.all_gather(weight_step, "fsdp", axis=0, tiled=True),
        lax.all_gather(weight_out, "fsdp", axis=0, tiled=True),
    )
    gain_all, gate_all, inner_all, shared_all, step_all, out_all = regathered
    gain_f = gain_all.astype(jnp.float32)
    cot_all = lax.all_gather(cotangent, "tp", axis=0, tiled=True)
    grad_out = weight_grad(cot_all, gated)
    grad_gated = jnp.dot(cot_all, out_all, preferred_element_type=jnp.float32)
    scaled = grad_gated * gain_gate
    grad_gategain = jnp.sum(grad_gated * mixed * inv_gate, axis=0)
    projection = lax.psum(jnp.sum(mixed * scaled, axis=1), "tp")
    grad_mixed = (
        inv_gate * scaled - mixed * (inv_gate * inv_gate * inv_gate) * (projection / INNER)[:, None]
    )
    (
        back_gate,
        back_inner,
        back_shared,
        back_step,
        back_filter,
        back_bias,
        back_offset,
        back_rate,
        back_skip,
    ) = pullback(grad_mixed)
    gate_low = back_gate.astype(jnp.bfloat16)
    inner_low = back_inner.astype(jnp.bfloat16)
    step_low = back_step.astype(jnp.bfloat16)
    shared_back = lax.psum_scatter(back_shared, "tp", scatter_dimension=0, tiled=True)
    shared_low = shared_back.astype(jnp.bfloat16)
    input_part = (
        transposed(gate_low, gate_all)
        + transposed(inner_low, inner_all)
        + transposed(step_low, step_all)
    )
    input_own = lax.psum_scatter(input_part, "tp", scatter_dimension=0, tiled=True)
    grad_normed = input_own + transposed(shared_low, shared_all)
    grad_gate_w = weight_grad(normed_all, gate_low)
    grad_inner_w = weight_grad(normed_all, inner_low)
    grad_step_w = weight_grad(normed_all, step_low)
    grad_shared_w = weight_grad(normed, shared_low)
    grad_gain = jnp.sum(grad_normed * x_hat, axis=0)
    scaled_in = grad_normed * gain_f[None, :]
    grad_hidden = cotangent.astype(jnp.float32) + inv_rms * (
        scaled_in - x_hat * jnp.mean(scaled_in * x_hat, axis=1, keepdims=True)
    )
    width_own = filter_inner.shape[1]
    fsdp_sums = (
        lax.psum_scatter(grad_gain, "fsdp", scatter_dimension=0, tiled=True),
        lax.psum_scatter(grad_gate_w, "fsdp", scatter_dimension=0, tiled=True),
        lax.psum_scatter(grad_inner_w, "fsdp", scatter_dimension=0, tiled=True),
        lax.psum_scatter(grad_shared_w, "fsdp", scatter_dimension=0, tiled=True),
        lax.psum_scatter(grad_step_w, "fsdp", scatter_dimension=0, tiled=True),
        lax.psum_scatter(grad_out, "fsdp", scatter_dimension=0, tiled=True),
    )
    small_sums = lax.psum(
        (
            back_filter[:, :width_own],
            back_bias[:width_own],
            back_offset,
            back_rate,
            back_skip,
            grad_gategain,
            back_filter[:, width_own:],
            back_bias[width_own:],
        ),
        "fsdp",
    )
    shared_sums = lax.psum((fsdp_sums[0], fsdp_sums[3], small_sums[6], small_sums[7]), "tp")
    return (
        layer_out,
        grad_hidden,
        shared_sums[0],
        fsdp_sums[1],
        fsdp_sums[2],
        shared_sums[1],
        fsdp_sums[4],
        small_sums[0],
        small_sums[1],
        shared_sums[2],
        shared_sums[3],
        small_sums[2],
        small_sums[3],
        small_sums[4],
        small_sums[5],
        fsdp_sums[5],
    )


def solution(mesh):
    return jax.shard_map(
        per_device,
        mesh=mesh,
        in_specs=(
            P(("fsdp", "tp"), None),
            P("fsdp"),
            P("fsdp", "tp"),
            P("fsdp", "tp"),
            P("fsdp", None),
            P("fsdp", "tp"),
            P(None, "tp"),
            P("tp"),
            P(),
            P(),
            P("tp"),
            P("tp"),
            P("tp"),
            P("tp"),
            P("fsdp", "tp"),
            P("fsdp", None),
            P(("fsdp", "tp"), None),
        ),
        out_specs=(
            P(("fsdp", "tp"), None),
            P(("fsdp", "tp"), None),
            P("fsdp"),
            P("fsdp", "tp"),
            P("fsdp", "tp"),
            P("fsdp", None),
            P("fsdp", "tp"),
            P(None, "tp"),
            P("tp"),
            P(),
            P(),
            P("tp"),
            P("tp"),
            P("tp"),
            P("tp"),
            P("fsdp", "tp"),
        ),
        check_vma=False,
    )
```

profile of v0, /device:TPU:0, one launch (start us, length us, event | category | flops | bytes accessed | tf_op | source)
XLA Modules:
  0.0 1209.7 jit_solution(5713207310811922395)
XLA Ops:
  10.1 34.9 %all-reduce.18 = bf16[1024]{0:T(1024)(128)(2,1)S(1)} all-reduce(bf16[1024]{0:T(1024)(128)(2,1)S(1)} %dynamic-update-slice), channel_id=1, replica_groups=mesh['fsdp'=16,'tp'=2] {'fsdp'}, use_global_device_ids=true, to_apply=%add.18 | all-reduce | flops 1024 | bytes 4096
  52.5 18.7 %all_gather.37 = bf16[1024,256]{1,0:T(8,128)(2,1)S(1)} all-gather(bf16[64,256]{1,0:T(8,128)(2,1)S(1)} %copy-done.39), channel_id=1, replica_groups=mesh['fsdp'=16,'tp'=2] {'fsdp'}, dimensions={0}, use_global_device_ids=true | all-gather | bytes 557056 | tf_op jit(solution)/shard_map/all_gather | solution.py:132
  73.7 11.9 all_gather.38
  85.9 21.6 %all-gather = bf16[16,64,16]{1,2,0:T(8,128)(2,1)S(1)} all-gather(bf16[1,64,16]{1,2,0:T(8,128)(2,1)S(1)} %bitcast.411), channel_id=1, replica_groups=mesh['fsdp'=16,'tp'=2] {'fsdp'}, dimensions={0}, use_global_device_ids=true | all-gather | bytes 34816 | tf_op jit(solution)/shard_map/all_gather | solution.py:133
  113.2 15.4 %all-gather.9.cloned.1.call-done = bf16[1024,1024]{1,0:T(8,128)(2,1)} async-done(((bf16[64,1024]{1,0:T(8,128)(2,1)}), bf16[1024,1024]{1,0:T(8,128)(2,1)}) %all-gather.9.cloned.1.call-update) | async-done | bytes 2097168 | tf_op jit(solution)/shard_map/all_gather | solution.py:131
  161.0 180.1 %while.45 = (s32[]{:T(128)}, f32[16,64,128]{2,1,0:T(8,128)S(1)}, s32[]{:T(128)}, f32[4,256,16,64]{1,0,3,2:T(4,128)}, f32[4,16,64,128]{3,2,1,0:T(8,128)}, /*index...) while((s32[]{:T(128)}, f32[16,64,128]{2,1,0:T(8,128)S(1)}, ...), condition=%wide.region_4.5_spmd.clone, body=%wide.region_1.4_spmd.clone.sunk | while | flops 1717654528 | bytes 13514427 | solution.py:59
  176.8 23.5 %dynamic_update_slice.85 = f32[4,256,16,64]{1,0,3,2:T(4,128)} dynamic-update-slice(f32[4,256,16,64]{1,0,3,2:T(4,128)} %get-tuple-element.1186, f32[1,256,16,64]{1,0,3,2:T(1,128)S(1)} %copy.298, s32[]{:T(128)} %get-tuple-element.1183, s32[]{:T(128)} %constant.136.clone.1..sunk, s32[]{:T(128)} %constant.136.clone.1..sunk, s32[]{:T(128)} %constant.136.clone.1..sunk) | dynamic-update-slice | bytes 2097156 | tf_op jit(solution)/shard_map/jvp()/while/body/jit(dynamic_update_index_in_dim)/dynamic_update_slice | solution.py:59
  221.8 23.4 %dynamic_update_slice.85 = f32[4,256,16,64]{1,0,3,2:T(4,128)} dynamic-update-slice(f32[4,256,16,64]{1,0,3,2:T(4,128)} %get-tuple-element.1186, f32[1,256,16,64]{1,0,3,2:T(1,128)S(1)} %copy.298, s32[]{:T(128)} %get-tuple-element.1183, s32[]{:T(128)} %constant.136.clone.1..sunk, s32[]{:T(128)} %constant.136.clone.1..sunk, s32[]{:T(128)} %constant.136.clone.1..sunk) | dynamic-update-slice | bytes 2097156 | tf_op jit(solution)/shard_map/jvp()/while/body/jit(dynamic_update_index_in_dim)/dynamic_update_slice | solution.py:59
  266.9 23.4 %dynamic_update_slice.85 = f32[4,256,16,64]{1,0,3,2:T(4,128)} dynamic-update-slice(f32[4,256,16,64]{1,0,3,2:T(4,128)} %get-tuple-element.1186, f32[1,256,16,64]{1,0,3,2:T(1,128)S(1)} %copy.298, s32[]{:T(128)} %get-tuple-element.1183, s32[]{:T(128)} %constant.136.clone.1..sunk, s32[]{:T(128)} %constant.136.clone.1..sunk, s32[]{:T(128)} %constant.136.clone.1..sunk) | dynamic-update-slice | bytes 2097156 | tf_op jit(solution)/shard_map/jvp()/while/body/jit(dynamic_update_index_in_dim)/dynamic_update_slice | solution.py:59
  311.9 23.4 %dynamic_update_slice.85 = f32[4,256,16,64]{1,0,3,2:T(4,128)} dynamic-update-slice(f32[4,256,16,64]{1,0,3,2:T(4,128)} %get-tuple-element.1186, f32[1,256,16,64]{1,0,3,2:T(1,128)S(1)} %copy.298, s32[]{:T(128)} %get-tuple-element.1183, s32[]{:T(128)} %constant.136.clone.1..sunk, s32[]{:T(128)} %constant.136.clone.1..sunk, s32[]{:T(128)} %constant.136.clone.1..sunk) | dynamic-update-slice | bytes 2097156 | tf_op jit(solution)/shard_map/jvp()/while/body/jit(dynamic_update_index_in_dim)/dynamic_update_slice | solution.py:59
  395.5 268.4 %while.46 = (s32[]{:T(128)}, f32[16,64,128]{2,1,0:T(8,128)}, f32[4,256,16,64]{1,0,3,2:T(4,128)}, f32[4,256,16]{1,0,2:T(4,128)}, f32[4,256,16]{1,0,2:T(4,128)}, /...) while((s32[]{:T(128)}, f32[16,64,128]{2,1,0:T(8,128)}, ...), condition=%wide.region_22.23_spmd.clone, body=%wide.region_10.22_spmd.clone.sunk | while | flops 3948037120 | bytes 37352084 | solution.py:59
  430.9 23.4 %dynamic_update_slice.89 = f32[4,256,16,64]{1,0,3,2:T(4,128)} dynamic-update-slice(f32[4,256,16,64]{1,0,3,2:T(4,128)} %get-tuple-element.1237, f32[1,256,16,64]{1,0,3,2:T(1,128)S(1)} %copy.307, s32[]{:T(128)S(6)} %sub.276, s32[]{:T(128)} %constant.136.clone.1..sunk.1, s32[]{:T(128)} %constant.136.clone.1..sunk.1, s32[]{:T(128)} %constant.136.clone.1..sunk.1) | dynamic-update-slice | bytes 2097156 | tf_op jit(solution)/shard_map/transpose(jvp())/while/body/jit(dynamic_update_index_in_dim)/dynamic_update_slice | solution.py:59
  498.1 23.4 %dynamic_update_slice.89 = f32[4,256,16,64]{1,0,3,2:T(4,128)} dynamic-update-slice(f32[4,256,16,64]{1,0,3,2:T(4,128)} %get-tuple-element.1237, f32[1,256,16,64]{1,0,3,2:T(1,128)S(1)} %copy.307, s32[]{:T(128)S(6)} %sub.276, s32[]{:T(128)} %constant.136.clone.1..sunk.1, s32[]{:T(128)} %constant.136.clone.1..sunk.1, s32[]{:T(128)} %constant.136.clone.1..sunk.1) | dynamic-update-slice | bytes 2097156 | tf_op jit(solution)/shard_map/transpose(jvp())/while/body/jit(dynamic_update_index_in_dim)/dynamic_update_slice | solution.py:59
  565.3 23.4 %dynamic_update_slice.89 = f32[4,256,16,64]{1,0,3,2:T(4,128)} dynamic-update-slice(f32[4,256,16,64]{1,0,3,2:T(4,128)} %get-tuple-element.1237, f32[1,256,16,64]{1,0,3,2:T(1,128)S(1)} %copy.307, s32[]{:T(128)S(6)} %sub.276, s32[]{:T(128)} %constant.136.clone.1..sunk.1, s32[]{:T(128)} %constant.136.clone.1..sunk.1, s32[]{:T(128)} %constant.136.clone.1..sunk.1) | dynamic-update-slice | bytes 2097156 | tf_op jit(solution)/shard_map/transpose(jvp())/while/body/jit(dynamic_update_index_in_dim)/dynamic_update_slice | solution.py:59
  632.5 23.4 %dynamic_update_slice.89 = f32[4,256,16,64]{1,0,3,2:T(4,128)} dynamic-update-slice(f32[4,256,16,64]{1,0,3,2:T(4,128)} %get-tuple-element.1237, f32[1,256,16,64]{1,0,3,2:T(1,128)S(1)} %copy.307, s32[]{:T(128)S(6)} %sub.276, s32[]{:T(128)} %constant.136.clone.1..sunk.1, s32[]{:T(128)} %constant.136.clone.1..sunk.1, s32[]{:T(128)} %constant.136.clone.1..sunk.1) | dynamic-update-slice | bytes 2097156 | tf_op jit(solution)/shard_map/transpose(jvp())/while/body/jit(dynamic_update_index_in_dim)/dynamic_update_slice | solution.py:59
  673.3 14.0 %multiply_reduce_fusion.6 = (f32[1280]{0:T(1024)S(1)}, f32[1280]{0:T(1024)S(1)}, f32[1280]{0:T(1024)S(1)}, f32[1280]{0:T(1024)S(1)}, f32[1280]{0:T(1024)S(1)}, /*index=5*/f32[1024,1280]{0,1:T(8,128)S(1)}) fusion(f32[1024,1280]{0,1:T(8,128)} %copy-done, f32[1024]{0:T(1024)S(1)} %copy-done.36, f32[1024]{0:T(1024)S(1)} %copy-done.34, f32[1024]{0:T(1024)S(1)} %copy-done.32, ...), kind=kLoop, calls=%fused_computation.156 | loop fusion | flops 35383040 | bytes 23630848 | tf_op jit(solution)/shard_map/transpose(jvp())/reduce_sum | solution.py:85
  696.7 18.9 %reduce-scatter.17.cloned.1.call-done = f32[512,256]{0,1:T(8,128)} async-done(((f32[1024,256]{0,1:T(8,128)}), f32[512,256]{0,1:T(8,128)}) %reduce-scatter.17.cloned.1.call-update) | async-done | bytes 524304 | tf_op jit(solution)/shard_map/reduce_scatter | solution.py:229
  739.5 38.2 %reduce-scatter.23.cloned.1.call-done = f32[64,256]{1,0:T(8,128)} async-done(((f32[1024,256]{1,0:T(8,128)}), f32[64,256]{1,0:T(8,128)}) %reduce-scatter.23.cloned.1.call-update) | async-done | bytes 65552 | tf_op jit(solution)/shard_map/reduce_scatter | solution.py:252
  804.7 32.0 %reduce-scatter.25.cloned.1.call-done = f32[64,16]{1,0:T(8,128)} async-done(((f32[1024,16]{1,0:T(8,128)}), f32[64,16]{1,0:T(8,128)}) %reduce-scatter.25.cloned.1.call-update) | async-done | bytes 4112
  838.1 54.3 %reduce-scatter.15.cloned.1.call-done = f32[512,1024]{1,0:T(8,128)} async-done(((f32[1024,1024]{1,0:T(8,128)}), f32[512,1024]{1,0:T(8,128)}) %reduce-scatter.15.cloned.1.call-update) | async-done | bytes 2097168 | tf_op jit(solution)/shard_map/reduce_scatter | solution.py:236
  895.4 61.9 %all-reduce.20 = (f32[1024]{0:T(1024)S(1)}, f32[4,1024]{1,0:T(4,128)}, f32[1024]{0:T(1024)}, f32[4,256]{1,0:T(4,128)S(1)}, f32[256]{0:T(256)S(1)}, /*index=5*/f3...) all-reduce(f32[1024]{0:T(1024)S(1)} %get-tuple-element.796, ...), channel_id=5, replica_groups=mesh['fsdp'=16,'tp'=2] {'fsdp'}, use_global_device_ids=true, to_apply=%region_27.28.clone | all-reduce | flops 8496 | bytes 67968
  972.0 77.2 %reduce-scatter.21.cloned.1.call-done = f32[64,1024]{1,0:T(8,128)} async-done(((f32[1024,1024]{1,0:T(8,128)}), f32[64,1024]{1,0:T(8,128)}) %reduce-scatter.21.cloned.1.call-update) | async-done | bytes 262160 | tf_op jit(solution)/shard_map/reduce_scatter | solution.py:251
  1049.2 76.0 %reduce-scatter.27.cloned.1.call-done = f32[64,1024]{1,0:T(8,128)} async-done(((f32[1024,1024]{1,0:T(8,128)}), f32[64,1024]{1,0:T(8,128)}) %reduce-scatter.27.cloned.1.call-update) | async-done | bytes 262160
  1125.2 76.3 %reduce-scatter.19.cloned.1.call-done = f32[64,1024]{1,0:T(8,128)} async-done(((f32[1024,1024]{1,0:T(8,128)}), f32[64,1024]{1,0:T(8,128)}) %reduce-scatter.19.cloned.1.call-update) | async-done | bytes 262160 | tf_op jit(solution)/shard_map/reduce_scatter | solution.py:250
  (520 shorter events, 442.6 us)
Async XLA Ops:
  7.2 102.5 %all-gather.7.cloned.1.call-start = ((), (), s32[]{:S(2)}) async-start(), calls=%async_computation.8 | async-start | bytes 3145728 | tf_op jit(solution)/shard_map/all_gather | solution.py:146
  46.6 62.9 %copy-start.56 = (bf16[16]{0:T(256)(128)(2,1)S(1)}, bf16[16]{0:T(256)(128)(2,1)}, u32[]{:S(2)}) copy-start(bf16[16]{0:T(256)(128)(2,1)} %param.33) | copy-start | bytes 100
  46.6 63.0 %copy-start.51 = (bf16[1024]{0:T(1024)(128)(2,1)S(1)}, bf16[1024]{0:T(1024)(128)(2,1)}, u32[]{:S(2)}) copy-start(bf16[1024]{0:T(1024)(128)(2,1)} %param.34) | copy-start | bytes 6148
  46.6 63.0 %copy-start.52 = (bf16[1024]{0:T(1024)(128)(2,1)S(1)}, bf16[1024]{0:T(1024)(128)(2,1)}, u32[]{:S(2)}) copy-start(bf16[1024]{0:T(1024)(128)(2,1)} %param.28) | copy-start | bytes 6148
  46.6 63.0 %copy-start.57 = (bf16[256]{0:T(256)(128)(2,1)S(1)}, bf16[256]{0:T(256)(128)(2,1)}, u32[]{:S(2)}) copy-start(bf16[256]{0:T(256)(128)(2,1)} %param.30) | copy-start | bytes 1540
  49.8 78.9 %all-gather.9.cloned.1.call-start = ((), (), s32[]{:S(2)}) async-start(), calls=%async_computation.9 | async-start | bytes 2228224 | tf_op jit(solution)/shard_map/all_gather | solution.py:131
  50.5 296.0 %all-gather.11.cloned.1.call-start = ((), (), s32[]{:S(2)}) async-start(), calls=%async_computation.10 | async-start | bytes 2228224 | tf_op jit(solution)/shard_map/all_gather | solution.py:130
  51.2 308.7 %all-gather.15.cloned.1.call-start = ((), (), s32[]{:S(2)}) async-start(), calls=%async_computation.13 | async-start | bytes 3145728 | tf_op jit(solution)/shard_map/all_gather | solution.py:206
  51.8 308.2 %all-gather.13.cloned.1.call-start = ((), (), s32[]{:S(2)}) async-start(), calls=%async_computation.11 | async-start | bytes 2228224 | tf_op jit(solution)/shard_map/all_gather | solution.py:134
  52.4 663.3 %reduce-scatter.17.cloned.1.call-start = ((), (), s32[]{:S(2)}) async-start(), calls=%async_computation.15 | async-start | bytes 1572864 | tf_op jit(solution)/shard_map/reduce_scatter | solution.py:229
  109.6 264.4 %copy-start.37 = (f32[1024]{0:T(1024)}, f32[1024]{0:T(1024)S(1)}, u32[]{:S(2)}) copy-start(f32[1024]{0:T(1024)S(1)} %mul.756) | copy-start | bytes 12292
  109.6 264.4 %copy-start.45 = (f32[1024]{0:T(1024)}, f32[1024]{0:T(1024)S(1)}, u32[]{:S(2)}) copy-start(f32[1024]{0:T(1024)S(1)} %convert_element_type.153) | copy-start | bytes 12292
  696.7 81.1 %reduce-scatter.23.cloned.1.call-start = ((), (), s32[]{:S(2)}) async-start(), calls=%async_computation.18 | async-start | bytes 1114112 | tf_op jit(solution)/shard_map/reduce_scatter | solution.py:252
  718.2 118.4 %reduce-scatter.25.cloned.1.call-start = ((), (), s32[]{:S(2)}) async-start(), calls=%async_computation.20 | async-start | bytes 557056
  720.3 172.1 %reduce-scatter.15.cloned.1.call-start = ((), (), s32[]{:S(2)}) async-start(), calls=%async_computation.14 | async-start | bytes 6291456 | tf_op jit(solution)/shard_map/reduce_scatter | solution.py:236
  731.2 231.7 %reduce-scatter.13.cloned.1.call-start = ((), (), s32[]{:S(2)}) async-start(), calls=%async_computation.12 | async-start | bytes 6291456 | tf_op jit(solution)/shard_map/reduce_scatter | solution.py:194
  739.5 232.5 %all-reduce.24.cloned.1.call-start = ((), (), s32[]{:S(2)}) async-start(), calls=%async_computation.19 | async-start | bytes 131072 | tf_op jit(solution)/shard_map/psum | solution.py:269
  777.8 271.4 %reduce-scatter.21.cloned.1.call-start = ((), (), s32[]{:S(2)}) async-start(), calls=%async_computation.17 | async-start | bytes 4456448 | tf_op jit(solution)/shard_map/reduce_scatter | solution.py:251
  784.5 340.7 %reduce-scatter.27.cloned.1.call-start = ((), (), s32[]{:S(2)}) async-start(), calls=%async_computation.21 | async-start | bytes 4456448
  797.5 403.9 %reduce-scatter.19.cloned.1.call-start = ((), (), s32[]{:S(2)}) async-start(), calls=%async_computation.16 | async-start | bytes 4456448 | tf_op jit(solution)/shard_map/reduce_scatter | solution.py:250
  803.5 88.9 %copy-start.5 = (bf16[512,1024]{1,0:T(8,128)(2,1)S(1)}, bf16[512,1024]{1,0:T(8,128)(2,1)}, u32[]{:S(2)}) copy-start(bf16[512,1024]{1,0:T(8,128)(2,1)} %param.21) | copy-start | bytes 3145732
  803.5 88.9 %copy-start.30 = (f32[1024]{0:T(1024)S(1)}, f32[1024]{0:T(1024)}, u32[]{:S(2)}) copy-start(f32[1024]{0:T(1024)} %copy-done.29) | copy-start | bytes 12292
  803.5 88.9 %copy-start.41 = (f32[512]{0:T(512)S(1)}, f32[512]{0:T(512)}, u32[]{:S(2)}) copy-start(f32[512]{0:T(512)} %copy-done.40) | copy-start | bytes 6148
  803.5 91.8 %copy-start.50 = (f32[1024]{0:T(1024)S(1)}, f32[1024]{0:T(1024)}, u32[]{:S(2)}) copy-start(f32[1024]{0:T(1024)} %get-tuple-element.792) | copy-start | bytes 12292
  (55 other events, 1080.2 us)
Sparse Core Ops, SparseCore 0:
  49.9 33.1 all-gather.6
  85.2 43.3 all-gather.8
  130.8 40.1 all-gather.10
  172.4 31.8 all-gather.14
  206.3 41.3 all-gather.12
  696.8 18.8 reduce-scatter.16
  720.3 57.4 reduce-scatter.22
  781.9 54.6 reduce-scatter.24
  839.1 53.3 reduce-scatter.14
  894.6 54.3 reduce-scatter.12
  951.3 20.7 all-reduce.23
  976.8 72.3 reduce-scatter.20
  1053.7 71.5 reduce-scatter.26
  1130.0 71.4 reduce-scatter.18
where the time goes:
time: 1220 us; the launch traced here: 1210 us
  waiting for transfers between devices  396 us (32%)
  local copies, waits for them, and re-layouts  330 us (27%)
  matrix products  204 us (17%)
  blocking collectives  164 us (13%)
  other arithmetic  86.6 us (7%)
  between operations  16.5 us (1%)
    dynamic_update_slice x36, local copies, waits for them, and re-layouts, block_scan(): unused, y_blocks = lax.scan(jax.checkpoint(block_step), initial, blocks_in)  214 us
    unnamed x16, waiting for transfers between devices  111 us
    unnamed x2, blocking collectives  96.8 us
    reduce_scatter x1, waiting for transfers between devices, per_device(): lax.psum_scatter(grad_inner_w, 'fsdp', scatter_dimension=0, tiled=True)  77.2 us
    reduce_scatter x1, waiting for transfers between devices, per_device(): lax.psum_scatter(grad_gate_w, 'fsdp', scatter_dimension=0, tiled=True)  76.3 us
    dot_general x12, matrix products, block_step(): y_block = jnp.einsum('tsh,shp->thp', mixing_w, x_blk, precision=HIGH)  65.3 us
    reduce_scatter x1, waiting for transfers between devices, per_device(): lax.psum_scatter(input_part, 'tp', scatter_dimension=0, tiled=True)  54.3 us
    reduce_scatter x1, waiting for transfers between devices, per_device(): lax.psum_scatter(grad_shared_w, 'fsdp', scatter_dimension=0, tiled=True)  38.2 us
  transfers between devices with their start and end apart: 14, of which 9 were waited for; matrix products, arithmetic and copies ran while one was open for 23% of the time, Pallas kernels for 0%

commit v1 on v0

v1 whole, which is shorter than its diff:
```python
import jax
import jax.numpy as jnp
from jax import lax
from jax.experimental import pallas as pl
from jax.experimental.pallas import tpu as pltpu
from jax.sharding import PartitionSpec as P

INNER = 2048
NS = 128
HEAD = 64
Q = 128
LOG2E = 1.4426950408889634
FAR = -1e30
EPSILON = 1e-05

F32 = jnp.float32
BF16 = jnp.bfloat16
HIGH = lax.Precision.HIGHEST


def mm(a, b):
    return jnp.dot(a, b, preferred_element_type=F32)


def mm_t(a, b):
    return lax.dot_general(a, b, (((1,), (1,)), ((), ())), preferred_element_type=F32)


def weight_grad(a, b):
    return lax.dot_general(a, b, (((0,), (0,)), ((), ())), preferred_element_type=F32)


def iota(shape, dim):
    return lax.broadcasted_iota(jnp.int32, shape, dim)


def softplus(v):
    return jnp.maximum(v, 0.0) + jnp.log1p(jnp.exp(-jnp.abs(v)))


def steps_of(step_ref, heads_ref):
    raw = step_ref[...].astype(F32) + heads_ref[0:1, :]
    dt = softplus(raw)
    lower = (iota((Q, Q), 0) >= iota((Q, Q), 1)).astype(F32)
    cum = jnp.dot(
        lower, dt * (heads_ref[1:2, :] * LOG2E), precision=HIGH, preferred_element_type=F32
    )
    return raw, dt, cum


def wide(column):
    return jnp.broadcast_to(column, (Q, 128))


def pair_of(first, array, pair):
    return jnp.where(
        first, wide(array[:, 2 * pair : 2 * pair + 1]), wide(array[:, 2 * pair + 1 : 2 * pair + 2])
    )


def stacked(first, block):
    nil = jnp.zeros_like(block)
    return jnp.concatenate([jnp.where(first, block, nil), jnp.where(first, nil, block)], axis=0)


def forward_kernel(
    turn_ref, u_ref, s_ref, step_ref, aux_ref, seg_ref, inner_ref, shared_ref, heads_ref,
    y_ref, conv_ref, convs_ref, states_ref,
    ubuf, sbuf, state,
):
    width = u_ref.shape[1]
    chunk = pl.program_id(0)

    @pl.when(chunk == 0)
    def _():
        ubuf[0:8, :] = jnp.zeros((8, width), F32)
        sbuf[0:8, :] = jnp.zeros((8, 2 * NS), F32)
        state[...] = jnp.zeros_like(state)

    @pl.when(chunk > 0)
    def _():
        ubuf[0:8, :] = ubuf[Q : Q + 8, :]
        sbuf[0:8, :] = sbuf[Q : Q + 8, :]

    ubuf[8 : Q + 8, :] = u_ref[...].astype(F32)
    sbuf[8 : Q + 8, :] = s_ref[...].astype(F32)
    aux = aux_ref[...]
    same = [wide(aux[:, k : k + 1]) for k in range(3)]
    keep = wide(aux[:, 6:7])
    tail_in = wide(aux[:, 7:8])

    def conv_of(buf, weights, cols):
        total = weights[4:5, cols] + weights[3:4, cols] * buf[8 : Q + 8, cols]
        for shift in range(1, 4):
            total = total + weights[3 - shift : 4 - shift, cols] * (
                buf[8 - shift : Q + 8 - shift, cols] * same[shift - 1]
            )
        return total

    def silu(v):
        return v * (0.5 + 0.5 * jnp.tanh(0.5 * v))

    conv_b = conv_of(sbuf, shared_ref, slice(0, NS))
    conv_c = conv_of(sbuf, shared_ref, slice(NS, 2 * NS))
    convs_ref[:, 0:NS] = conv_b
    convs_ref[:, NS : 2 * NS] = conv_c
    b_f = silu(conv_b)
    b_low = b_f.astype(BF16)
    b_turn = b_f.T.astype(BF16)
    c_low = silu(conv_c).astype(BF16)
    inner_cb = mm_t(c_low, b_low)
    visible = (wide(aux[:, 8:9]) == seg_ref[0]) & (iota((Q, Q), 0) >= iota((Q, Q), 1))
    bias = jnp.where(visible, 0.0, FAR)
    raw, dt, cum = steps_of(step_ref, heads_ref)
    cum_t = cum.T
    first = iota((Q, 128), 1) < HEAD
    for pair in range(width // 128):
        cols = slice(128 * pair, 128 * pair + 128)
        conv = conv_of(ubuf, inner_ref, cols)
        conv_ref[:, cols] = conv
        x = silu(conv)
        cum_1 = wide(cum[:, 2 * pair : 2 * pair + 1])
        cum_2 = wide(cum[:, 2 * pair + 1 : 2 * pair + 2])
        m_1 = inner_cb * jnp.exp2(cum_1 - cum_t[2 * pair : 2 * pair + 1, :] + bias)
        m_2 = inner_cb * jnp.exp2(cum_2 - cum_t[2 * pair + 1 : 2 * pair + 2, :] + bias)
        xd = x * pair_of(first, dt, pair)
        mixers = jnp.concatenate([m_1.astype(BF16), m_2.astype(BF16)], axis=1)
        y = mm(mixers, stacked(first, xd.astype(BF16)))
        cum_p = jnp.where(first, cum_1, cum_2)
        last = cum_p[Q - 1 : Q, :]
        old = state[:, cols]
        old_low = old.astype(BF16)
        states_ref[0, :, cols] = old_low
        y = y + mm(c_low, old_low) * (jnp.exp2(cum_p) * keep)
        y_ref[:, cols] = y + inner_ref[5:6, cols] * x
        tail = jnp.exp2(last - cum_p) * tail_in
        carry = jnp.exp2(last) * keep[Q - 1 : Q, :]
        state[:, cols] = old * carry + mm(b_turn, (xd * tail).astype(BF16))


def backward_kernel(
    turn_ref, u_ref, s_ref, conv_ref, convs_ref, step_ref, aux_ref, seg_ref, grad_ref, states_ref,
    inner_ref, shared_ref, heads_ref,
    low_ref, inner_sum, shared_sum, heads_sum,
    dbuf, dsbuf, dstate, dcum_t, red, wgrad, xtail,
):
    width = u_ref.shape[1]
    chunk = pl.program_id(0)

    @pl.when(chunk == 0)
    def _():
        dbuf[Q : Q + 8, :] = jnp.zeros((8, width), F32)
        dsbuf[Q : Q + 8, :] = jnp.zeros((8, 2 * NS), F32)
        dstate[...] = jnp.zeros_like(dstate)
        dcum_t[...] = jnp.zeros_like(dcum_t)
        inner_sum[...] = jnp.zeros_like(inner_sum)
        shared_sum[...] = jnp.zeros_like(shared_sum)
        heads_sum[...] = jnp.zeros_like(heads_sum)

    @pl.when(chunk > 0)
    def _():
        dbuf[Q : Q + 8, :] = dbuf[0:8, :]
        dsbuf[Q : Q + 8, :] = dsbuf[0:8, :]

    aux = aux_ref[...]
    same = [wide(aux[:, 3 + k : 4 + k]) for k in range(3)]
    keep = wide(aux[:, 6:7])
    tail_in = wide(aux[:, 7:8])

    def silu_and_slope(v):
        sig = 0.5 + 0.5 * jnp.tanh(0.5 * v)
        act = v * sig
        return act, sig + act * (1.0 - sig)

    b_f, b_slope = silu_and_slope(convs_ref[:, 0:NS])
    c_f, c_slope = silu_and_slope(convs_ref[:, NS : 2 * NS])
    b_low = b_f.astype(BF16)
    c_low = c_f.astype(BF16)
    c_turn = c_f.T.astype(BF16)
    inner_bc = mm_t(b_low, c_low)
    row, column = iota((Q, Q), 0), iota((Q, Q), 1)
    visible = (wide(aux[:, 8:9]) == seg_ref[0]) & (row <= column)
    bias = jnp.where(visible, 0.0, FAR)
    lower_low = (row >= column).astype(BF16)
    strict = row < column
    raw, dt, cum = steps_of(step_ref, heads_ref)
    cum_t = cum.T
    first = iota((Q, 128), 1) < HEAD
    dinner = jnp.zeros((Q, Q), F32)
    for pair in range(width // 128):
        cols = slice(128 * pair, 128 * pair + 128)
        cum_1 = wide(cum[:, 2 * pair : 2 * pair + 1])
        cum_2 = wide(cum[:, 2 * pair + 1 : 2 * pair + 2])
        decay_1 = jnp.exp2(cum_t[2 * pair : 2 * pair + 1, :] - cum_1 + bias)
        decay_2 = jnp.exp2(cum_t[2 * pair + 1 : 2 * pair + 2, :] - cum_2 + bias)
        m_1 = inner_bc * decay_1
        m_2 = inner_bc * decay_2
        x, slope = silu_and_slope(conv_ref[:, cols])
        dt_p = pair_of(first, dt, pair)
        xd = x * dt_p
        grad = grad_ref[:, cols].astype(F32)
        grad_low = grad.astype(BF16)
        dm = mm_t(stacked(first, xd.astype(BF16)), grad_low)
        dm_1, dm_2 = dm[0:Q, :], dm[Q : 2 * Q, :]
        dinner = dinner + dm_1 * decay_1 + dm_2 * decay_2
        gaps = jnp.concatenate([(dm_1 * m_1).astype(BF16), (dm_2 * m_2).astype(BF16)], axis=0)
        spans = mm(gaps, lower_low)
        dcum_t[2 * pair : 2 * pair + 1, :] = jnp.sum(
            jnp.where(strict, spans[0:Q, :], 0.0), axis=0, keepdims=True
        )
        dcum_t[2 * pair + 1 : 2 * pair + 2, :] = jnp.sum(
            jnp.where(strict, spans[Q : 2 * Q, :], 0.0), axis=0, keepdims=True
        )
        mixers = jnp.concatenate([m_1.astype(BF16), m_2.astype(BF16)], axis=1)
        dxd = mm(mixers, stacked(first, grad_low))
        cum_p = jnp.where(first, cum_1, cum_2)
        last = cum_p[Q - 1 : Q, :]
        tail = jnp.exp2(last - cum_p) * tail_in
        later = dstate[:, cols]
        old_low = states_ref[0, :, cols]
        xt = xd * tail
        from_end = mm(b_low, later.astype(BF16))
        dxd = dxd + tail * from_end
        weight = jnp.exp2(cum_p) * keep
        wg = grad * weight
        from_start = mm(c_low, old_low)
        carry = jnp.exp2(last) * keep[Q - 1 : Q, :]
        carried = jnp.sum(later * old_low.astype(F32), axis=0, keepdims=True) * carry
        red[0:Q, cols] = (dxd * x).astype(BF16)
        red[Q : 2 * Q, cols] = (xt * from_end).astype(BF16)
        red[2 * Q : 3 * Q, cols] = (wg * from_start).astype(BF16)
        red[3 * Q : 3 * Q + 16, cols] = jnp.broadcast_to(carried, (16, 128)).astype(BF16)
        wg_low = wg.astype(BF16)
        wgrad[:, cols] = wg_low
        xtail[:, cols] = xt.astype(BF16)
        dx = dxd * dt_p + inner_ref[5:6, cols] * grad
        dbuf[0:Q, cols] = dx * slope
        inner_sum[5:6, cols] += jnp.sum(grad * x, axis=0, keepdims=True)

    to_head = (iota((width, 128), 0) // HEAD == iota((width, 128), 1)).astype(BF16)
    sums = mm(red[...], to_head)
    lower = (row >= column).astype(F32)
    upper = (row <= column).astype(F32)
    strict_lower = (row > column).astype(F32)
    dla = (
        dcum_t[...].T
        + jnp.dot(strict_lower, sums[Q : 2 * Q, :], precision=HIGH, preferred_element_type=F32)
        + jnp.dot(upper, sums[2 * Q : 3 * Q, :], precision=HIGH, preferred_element_type=F32)
        + sums[3 * Q : 3 * Q + 1, :]
    )
    rate = heads_ref[1:2, :]
    ddt = sums[0:Q, :] + rate * dla
    dstep = ddt * (0.5 + 0.5 * jnp.tanh(0.5 * raw))
    low_ref[:, width + 2 * NS : width + 2 * NS + 128] = dstep.astype(BF16)
    heads_sum[0:1, :] += jnp.sum(dstep, axis=0, keepdims=True)
    heads_sum[1:2, :] += jnp.sum(dla * dt * rate, axis=0, keepdims=True)

    dinner_low = dinner.astype(BF16)
    later_low = dstate[...].astype(BF16)
    db = mm(dinner_low, c_low) + mm_t(xtail[...], later_low)
    dc = mm(dinner.T.astype(BF16), b_low) + mm_t(wgrad[...], states_ref[0])
    dsbuf[0:Q, 0:NS] = db * b_slope
    dsbuf[0:Q, NS : 2 * NS] = dc * c_slope

    def conv_back(u, buf, weights, sums_ref, cols):
        d = buf[0:Q, cols]
        du = weights[3:4, cols] * d
        sums_ref[3:4, cols] += jnp.sum(d * u, axis=0, keepdims=True)
        sums_ref[4:5, cols] += jnp.sum(d, axis=0, keepdims=True)
        for shift in range(1, 4):
            d = buf[shift : Q + shift, cols] * same[shift - 1]
            du = du + weights[3 - shift : 4 - shift, cols] * d
            sums_ref[3 - shift : 4 - shift, cols] += jnp.sum(d * u, axis=0, keepdims=True)
        return du

    for part in range(2):
        cols = slice(NS * part, NS * part + NS)
        low_ref[:, width + NS * part : width + NS * part + NS] = conv_back(
            s_ref[:, cols].astype(F32), dsbuf, shared_ref, shared_sum, cols
        ).astype(BF16)
    new = mm(c_turn, wgrad[...])
    for pair in range(width // 128):
        cols = slice(128 * pair, 128 * pair + 128)
        low_ref[:, cols] = conv_back(
            u_ref[:, cols].astype(F32), dbuf, inner_ref, inner_sum, cols
        ).astype(BF16)
        cum_p = jnp.where(
            first[0:1, :],
            jnp.broadcast_to(cum[Q - 1 : Q, 2 * pair : 2 * pair + 1], (1, 128)),
            jnp.broadcast_to(cum[Q - 1 : Q, 2 * pair + 1 : 2 * pair + 2], (1, 128)),
        )
        carry = jnp.exp2(cum_p) * keep[Q - 1 : Q, :]
        dstate[:, cols] = dstate[:, cols] * carry + new[:, cols]


VMEM_LIMIT = 48 * 1024 * 1024


def forward_mix(turn, proj, aux, seg_rows, inner_p, shared_p, heads_p):
    length = proj.shape[0]
    width = inner_p.shape[1]
    chunks = length // Q

    def rows(n, at=0):
        return pl.BlockSpec((Q, n), lambda c, turn: (lax.rem(c + turn[0], chunks), at))

    def plain(n):
        return pl.BlockSpec((Q, n), lambda c, turn: (c, 0))

    def whole(n):
        return pl.BlockSpec((8, n), lambda c, turn: (0, 0))

    line = pl.BlockSpec((1, 1, Q), lambda c, turn: (c, 0, 0))
    kept = pl.BlockSpec((1, NS, width), lambda c, turn: (c, 0, 0))
    return pl.pallas_call(
        forward_kernel,
        grid_spec=pltpu.PrefetchScalarGridSpec(
            num_scalar_prefetch=1,
            grid=(chunks,),
            in_specs=[
                rows(width), rows(2 * NS, width // (2 * NS)), rows(128, (width + 2 * NS) // 128),
                plain(16), line, whole(width), whole(2 * NS), whole(128),
            ],
            out_specs=[rows(width), plain(width), plain(2 * NS), kept],
            scratch_shapes=[
                pltpu.VMEM((Q + 8, width), F32),
                pltpu.VMEM((Q + 8, 2 * NS), F32),
                pltpu.VMEM((NS, width), F32),
            ],
        ),
        out_shape=[
            jax.ShapeDtypeStruct((length, width), F32),
            jax.ShapeDtypeStruct((length, width), F32),
            jax.ShapeDtypeStruct((length, 2 * NS), F32),
            jax.ShapeDtypeStruct((chunks, NS, width), BF16),
        ],
        compiler_params=pltpu.CompilerParams(vmem_limit_bytes=VMEM_LIMIT),
        cost_estimate=pl.CostEstimate(
            flops=32 * length * 128 * width, bytes_accessed=12 * length * width, transcendentals=0
        ),
        name="mix_forward",
    )(turn, proj, proj, proj, aux, seg_rows, inner_p, shared_p, heads_p)


def backward_mix(turn, proj, conv, convs, aux, seg_rows, grad, states, inner_p, shared_p, heads_p):
    length = proj.shape[0]
    width = inner_p.shape[1]
    chunks = length // Q

    def rows(n, at=0):
        return pl.BlockSpec(
            (Q, n), lambda c, turn: (lax.rem(chunks - 1 - c + turn[0], chunks), at)
        )

    def plain(n):
        return pl.BlockSpec((Q, n), lambda c, turn: (chunks - 1 - c, 0))

    def whole(n):
        return pl.BlockSpec((8, n), lambda c, turn: (0, 0))

    line = pl.BlockSpec((1, 1, Q), lambda c, turn: (chunks - 1 - c, 0, 0))
    kept = pl.BlockSpec((1, NS, width), lambda c, turn: (chunks - 1 - c, 0, 0))
    return pl.pallas_call(
        backward_kernel,
        grid_spec=pltpu.PrefetchScalarGridSpec(
            num_scalar_prefetch=1,
            grid=(chunks,),
            in_specs=[
                rows(width), rows(2 * NS, width // (2 * NS)), plain(width), plain(2 * NS),
                rows(128, (width + 2 * NS) // 128), plain(16), line, rows(width), kept,
                whole(width), whole(2 * NS), whole(128),
            ],
            out_specs=[rows(width + 2 * NS + 128), whole(width), whole(2 * NS), whole(128)],
            scratch_shapes=[
                pltpu.VMEM((Q + 8, width), F32),
                pltpu.VMEM((Q + 8, 2 * NS), F32),
                pltpu.VMEM((NS, width), F32),
                pltpu.VMEM((128, Q), F32),
                pltpu.VMEM((3 * Q + 16, width), BF16),
                pltpu.VMEM((Q, width), BF16),
                pltpu.VMEM((Q, width), BF16),
            ],
        ),
        out_shape=[
            jax.ShapeDtypeStruct((length, width + 2 * NS + 128), BF16),
            jax.ShapeDtypeStruct((8, width), F32),
            jax.ShapeDtypeStruct((8, 2 * NS), F32),
            jax.ShapeDtypeStruct((8, 128), F32),
        ],
        compiler_params=pltpu.CompilerParams(vmem_limit_bytes=VMEM_LIMIT),
        cost_estimate=pl.CostEstimate(
            flops=70 * length * 128 * width, bytes_accessed=20 * length * width, transcendentals=0
        ),
        name="mix_backward",
    )(turn, proj, proj, conv, convs, proj, aux, seg_rows, grad, states, inner_p, shared_p, heads_p)


def aux_of(seg_line):
    length = seg_line.shape[0]
    ends = seg_line.reshape(-1, Q)[:, Q - 1]
    prior = jnp.concatenate([jnp.full((1,), -1, seg_line.dtype), ends[:-1]])
    place = jnp.arange(length)
    columns = []
    for shift in range(1, 4):
        columns.append((jnp.roll(seg_line, shift) == seg_line) & (place >= shift))
    for shift in range(1, 4):
        columns.append((jnp.roll(seg_line, -shift) == seg_line) & (place < length - shift))
    columns.append(seg_line == jnp.repeat(prior, Q))
    columns.append(seg_line == jnp.repeat(ends, Q))
    columns = [column.astype(F32) for column in columns] + [seg_line.astype(F32)]
    columns += [jnp.zeros((length,), F32)] * (16 - len(columns))
    rows = seg_line.astype(F32).reshape(-1, 1, Q)
    return jnp.stack(columns, axis=1), rows


def silu_of(v):
    return v * jax.nn.sigmoid(v)


def program(sizes, args):
    (
        hidden, norm_gain, weight_gate, weight_inner, weight_shared, weight_step,
        filter_inner, bias_inner, filter_shared, bias_shared, step_bias, log_rate, skip_gain,
        gate_gain, weight_out, segments, cotangent,
    ) = args
    n_fsdp, n_tp = sizes
    width = weight_gate.shape[1]
    heads = weight_step.shape[1]
    own_rows = hidden.shape[0]
    length = segments.shape[1]
    tp_place = lax.axis_index("tp")
    paired = n_tp == 2

    def tp_rows(own):
        if paired:
            return jnp.concatenate([own, lax.ppermute(own, "tp", [(0, 1), (1, 0)])], axis=0)
        return lax.all_gather(own, "tp", axis=0, tiled=True)

    def tp_scatter(part):
        if paired:
            away = lax.ppermute(part[own_rows:].astype(BF16), "tp", [(0, 1), (1, 0)])
            return part[:own_rows] + away.astype(F32)
        return lax.psum_scatter(part, "tp", scatter_dimension=0, tiled=True)

    def gather(shard):
        return lax.all_gather(shard, "fsdp", axis=0, tiled=True)

    def scatter(total):
        return lax.psum_scatter(total, "fsdp", scatter_dimension=0, tiled=True).astype(F32)

    def butterfly(value):
        reach = 1
        while reach < n_fsdp:
            value = value + lax.ppermute(
                value, "fsdp", [(i, i ^ reach) for i in range(n_fsdp)]
            )
            reach *= 2
        return value

    pad = jnp.zeros((weight_step.shape[0], 128 - heads - 1), BF16)
    shard_a = jnp.concatenate(
        [weight_inner, weight_shared, weight_step, norm_gain[:, None], pad], axis=1
    )
    shard_b = jnp.concatenate([weight_gate, weight_out], axis=1)
    hidden_all = tp_rows(hidden)
    weights_a = gather(shard_a)
    cot_all = tp_rows(cotangent)
    weights_b = gather(shard_b)
    gate_all, out_all = weights_b[:, :width], weights_b[:, width:]
    gain_row = weights_a[:, width + 2 * NS + heads].astype(F32)[None, :]

    hidden_f = hidden_all.astype(F32)
    inv_rms = lax.rsqrt(jnp.mean(hidden_f * hidden_f, axis=1, keepdims=True) + EPSILON)
    normed = (hidden_f * inv_rms * gain_row).astype(BF16)
    proj = mm(normed, weights_a).astype(BF16)

    turn = (tp_place * (own_rows // Q) if paired else jnp.zeros((), jnp.int32)).reshape(1)
    turn = turn.astype(jnp.int32)
    aux, seg_rows = aux_of(segments[0])
    skip_lanes = jnp.repeat(skip_gain.astype(F32), HEAD)
    inner_p = jnp.concatenate(
        [filter_inner.astype(F32), bias_inner.astype(F32)[None], skip_lanes[None],
         jnp.zeros((2, width), F32)], axis=0)
    shared_p = jnp.concatenate(
        [filter_shared.astype(F32), bias_shared.astype(F32)[None], jnp.zeros((3, 2 * NS), F32)],
        axis=0,
    )
    heads_p = jnp.pad(
        jnp.stack([step_bias.astype(F32), -jnp.exp(log_rate.astype(F32))]),
        ((0, 6), (0, 128 - heads)),
    )
    y, conv, convs, states = forward_mix(turn, proj, aux, seg_rows, inner_p, shared_p, heads_p)

    gate_z = mm(normed, gate_all).astype(BF16).astype(F32)
    grad_gated = mm(cot_all, out_all)
    gain_gate = gate_gain.astype(F32)[None, :]
    sig = jax.nn.sigmoid(gate_z)
    act = gate_z * sig
    mixed = y * act
    scaled = grad_gated * gain_gate
    sums = jnp.stack([jnp.sum(mixed * mixed, axis=1), jnp.sum(mixed * scaled, axis=1)], axis=1)
    if paired:
        half = jnp.concatenate([sums[own_rows:], sums[:own_rows]], axis=0)
        sums = sums + lax.ppermute(half, "tp", [(0, 1), (1, 0)])
    else:
        sums = lax.psum(sums, "tp")
    inv_gate = lax.rsqrt(sums[:, 0:1] / INNER + EPSILON)
    gated = (mixed * inv_gate * gain_gate).astype(BF16)
    grad_mixed = inv_gate * scaled - mixed * (inv_gate * inv_gate * inv_gate) * (
        sums[:, 1:2] / INNER
    )
    grad_y = grad_mixed * act
    low_z = (grad_mixed * y * (sig + act * (1.0 - sig))).astype(BF16)
    grad_gain_gate = jnp.sum(grad_gated * mixed * inv_gate, axis=0)
    grads_b = jnp.concatenate(
        [weight_grad(normed, low_z), weight_grad(cot_all, gated)], axis=1
    ).astype(BF16)
    owned_b = scatter(grads_b)
    out_own = tp_scatter(mm_t(gated, out_all))
    layer_out = (hidden.astype(F32) + out_own).astype(BF16)

    low, inner_sum, shared_sum, heads_sum = backward_mix(
        turn, proj, conv, convs, aux, seg_rows, grad_y, states, inner_p, shared_p, heads_p
    )
    grads_a = weight_grad(normed, low).astype(BF16)
    owned_a = scatter(grads_a)
    small = butterfly(
        jnp.concatenate(
            [jnp.concatenate([inner_sum[:6], grad_gain_gate[None], inner_sum[7:]], axis=0),
             shared_sum, heads_sum], axis=1)
    )
    grad_normed = tp_scatter(mm_t(low_z, gate_all) + mm_t(low, weights_a))
    x_hat = hidden.astype(F32) * inv_rms[:own_rows] if paired else None
    inv_own = inv_rms[:own_rows]
    if not paired:
        inv_own = lax.dynamic_slice_in_dim(inv_rms, tp_place * own_rows, own_rows, 0)
        x_hat = hidden.astype(F32) * inv_own
    scaled_in = grad_normed * gain_row
    grad_hidden = cotangent.astype(F32) + inv_own * (
        scaled_in - x_hat * jnp.mean(scaled_in * x_hat, axis=1, keepdims=True)
    )

    grad_gate, grad_out = owned_b[:, :width], owned_b[:, width:]
    grad_inner = owned_a[:, :width]
    grad_shared = owned_a[:, width : width + 2 * NS]
    grad_step = owned_a[:, width + 2 * NS : width + 2 * NS + heads]
    gain_own = (
        jnp.sum(weight_gate.astype(F32) * grad_gate, axis=1)
        + jnp.sum(weight_inner.astype(F32) * grad_inner, axis=1)
        + jnp.sum(weight_shared.astype(F32) * grad_shared, axis=1)
        + jnp.sum(weight_step.astype(F32) * grad_step, axis=1)
    )
    shared_part = small[:, width : width + 2 * NS]
    grad_shared, gain_own, shared_part = lax.psum((grad_shared, gain_own, shared_part), "tp")
    grad_norm_gain = gain_own / norm_gain.astype(F32)
    head_part = small[:, width + 2 * NS :]
    return (
        layer_out,
        grad_hidden,
        grad_norm_gain,
        grad_gate,
        grad_inner,
        grad_shared,
        grad_step,
        small[0:4, :width],
        small[4, :width],
        shared_part[0:4],
        shared_part[4],
        head_part[0, :heads],
        head_part[1, :heads],
        jnp.sum(small[5, :width].reshape(heads, HEAD), axis=1),
        small[6, :width],
        grad_out,
    )


def solution(mesh):
    sizes = (mesh.shape["fsdp"], mesh.shape["tp"])

    def per_device(*args):
        return program(sizes, args)

    return jax.shard_map(
        per_device,
        mesh=mesh,
        in_specs=(
            P(("fsdp", "tp"), None),
            P("fsdp"),
            P("fsdp", "tp"),
            P("fsdp", "tp"),
            P("fsdp", None),
            P("fsdp", "tp"),
            P(None, "tp"),
            P("tp"),
            P(),
            P(),
            P("tp"),
            P("tp"),
            P("tp"),
            P("tp"),
            P("fsdp", "tp"),
            P("fsdp", None),
            P(("fsdp", "tp"), None),
        ),
        out_specs=(
            P(("fsdp", "tp"), None),
            P(("fsdp", "tp"), None),
            P("fsdp"),
            P("fsdp", "tp"),
            P("fsdp", "tp"),
            P("fsdp", None),
            P("fsdp", "tp"),
            P(None, "tp"),
            P("tp"),
            P(),
            P(),
            P("tp"),
            P("tp"),
            P("tp"),
            P("tp"),
            P("fsdp", "tp"),
        ),
        check_vma=False,
    )
```

time: 1220 us -> 351 us (0.29)
  local copies, waits for them, and re-layouts: 330 us -> 38.9 us
  waiting for transfers between devices: 396 us -> 153 us
  blocking collectives: 164 us -> 5.07 us
  matrix products: 204 us -> 49.9 us
  other arithmetic: 86.6 us -> 31 us
  Pallas kernels: 0 us -> 47.2 us
    reduce_scatter x6 -> x0, waiting for transfers between devices: 265 us -> none  [the longest x1 77.2 us: per_device(): lax.psum_scatter(grad_inner_w, 'fsdp', scatter_dimension=0, tiled=True)]
    dynamic_update_slice x36 -> x0, local copies, waits for them, and re-layouts: 214 us -> none  [block_scan(): unused, y_blocks = lax.scan(jax.checkpoint(block_step), initial, blocks_in)]
    dot_general x70 -> x9, matrix products: 202 us -> 49.9 us  [the longest x3 18.9 us: weight_grad(): lax.dot_general(a, b, (((0,), (0,)), ((), ())), preferred_element_type=F32)]
    unnamed x2 -> x0, blocking collectives: 96.8 us -> none
    ppermute x0 -> x9, waiting for transfers between devices: none -> 59.6 us  [the longest x2 26.9 us: tp_rows(): lax.ppermute(own, 'tp', [(0, 1), (1, 0)])]
    all_gather x3 -> x0, blocking collectives: 52.3 us -> none  [the longest x1 21.6 us: per_device(): lax.all_gather(weight_step, 'fsdp', axis=0, tiled=True)]
    pallas_call x0 -> x2, Pallas kernels: none -> 47.2 us  [the longest x1 33.2 us: backward_mix(): pl.pallas_call(backward_kernel, grid_spec=pltpu.PrefetchScalarGridSpec(nu...]
    unnamed x16 -> x7, waiting for transfers between devices: 111 us -> 71.7 us
  transfers between devices with their start and end apart: 14 -> 14, of which waited for: 9 -> 9; matrix products, arithmetic and copies ran while one was open for 23% -> 25% of each run, Pallas kernels for 0% -> 4%
where the time goes in v1:
time: 351 us; the launch traced here: 350 us
  waiting for transfers between devices  153 us (44%)
  matrix products  49.9 us (14%)
  Pallas kernels  47.2 us (13%)
  local copies, waits for them, and re-layouts  38.9 us (11%)
  other arithmetic  31 us (9%)
  between operations  14.3 us (4%)
  starting transfers between devices  10.3 us (3%)
  blocking collectives  5.07 us (1%)
    unnamed x7, waiting for transfers between devices  71.7 us
    pallas_call x1, Pallas kernels, backward_mix(): pl.pallas_call(backward_kernel, grid_spec=pltpu.PrefetchScalarGridSpec(nu...  33.2 us
    ppermute x2, waiting for transfers between devices, tp_rows(): lax.ppermute(own, 'tp', [(0, 1), (1, 0)])  26.9 us
    ppermute x2, waiting for transfers between devices, tp_scatter(): away = lax.ppermute(part[own_rows:].astype(BF16), 'tp', [(0, 1), (1, 0)])  26.4 us
    all_gather x2, waiting for transfers between devices, gather(): return lax.all_gather(shard, 'fsdp', axis=0, tiled=True)  22.2 us
    dot_general x3, matrix products, weight_grad(): lax.dot_general(a, b, (((0,), (0,)), ((), ())), preferred_element_type=F32)  18.9 us
    dot_general x3, matrix products, mm(): return jnp.dot(a, b, preferred_element_type=F32)  18.2 us
    unnamed x68, local copies, waits for them, and re-layouts  18 us
  transfers between devices with their start and end apart: 14, of which 9 were waited for; matrix products, arithmetic and copies ran while one was open for 25% of the time, Pallas kernels for 4%

profile of v1, /device:TPU:0, one launch (start us, length us, event | category | flops | bytes accessed | tf_op | source)
XLA Modules:
  0.0 349.9 jit_solution(888796075025016498)
XLA Ops:
  33.9 5.6 %collective-permute-done = bf16[512,1024]{1,0:T(8,128)(2,1)S(1)} collective-permute-done((bf16[512,1024]{1,0:T(8,128)(2,1)}, bf16[512,1024]{1,0:T(8,128)(2,1)S(1)}, u32[]{:S(2)}, u32[]{:S(2)}) %collective-permute-start) | collective-permute-done | bytes 1048608 | tf_op jit(solution)/shard_map/ppermute | solution.py:436
  40.1 21.3 %collective-permute-done.1 = bf16[512,1024]{1,0:T(8,128)(2,1)} collective-permute-done((bf16[512,1024]{1,0:T(8,128)(2,1)}, bf16[512,1024]{1,0:T(8,128)(2,1)}, u32[]{:S(2)}, u32[]{:S(2)}) %collective-permute-start.1) | collective-permute-done | bytes 1048608 | tf_op jit(solution)/shard_map/ppermute | solution.py:436
  64.8 8.0 %convolution_convert_fusion.1.u_ref.s_ref.step_ref = bf16[1024,1408]{1,0:T(8,128)(2,1)} fusion(bf16[1024,1408]{1,0:T(8,128)(2,1)} %all-gather.3.cloned.1.call-done, f32[1024]{0:T(1024)S(1)} %convert_reduce_fusion, f32[1024]{0:T(1024)S(1)} %add_rsqrt_fusion, bf16[512,1024]{1,0:T(8,128)(2,1)S(1)} %collective-permute-done, bf16[512,1024]{1,0:T(8,128)(2,1)S(1)} %copy-done.2), kind=kOutput, calls=%fused_computation.18 | convolution fusion | flops 2961571840 | bytes 7872512 | tf_op jit(solution)/shard_map/dot_general | solution.py:22
  72.8 13.9 %mix_forward.1 = (f32[1024,1024]{1,0:T(8,128)}, f32[1024,1024]{1,0:T(8,128)}, f32[1024,256]{1,0:T(8,128)S(1)}, bf16[8,128,1024]{2,1,0:T(8,128)(2,1)S(1)}) custom-call(s32[1]{0:T(128)} %bitcast.turn_ref, bf16[1024,1408]{1,0:T(8,128)(2,1)} %convolution_convert_fusion.1.u_ref.s_ref.step_ref, bf16[1024,1408]{1,0:T(8,128)(2,1)} %convolution_convert_fusion.1.u_ref.s_ref.step_ref, ...), custom_call_target="tpu_custom_call" | custom-call | flops 4294967296 | bytes 12582912 | tf_op jit(solution)/shard_map/mix_forward/pallas_call | solution.py:315
  87.7 22.2 %all-gather.5.cloned.1.call-done = bf16[1024,2048]{1,0:T(8,128)(2,1)} async-done(((bf16[64,2048]{1,0:T(8,128)(2,1)}), bf16[1024,2048]{1,0:T(8,128)(2,1)}) %all-gather.5.cloned.1.call-update) | async-done | bytes 4194320 | tf_op jit(solution)/shard_map/all_gather | solution.py:446
  109.9 4.7 %convolution_convert_fusion.4 = bf16[1024,1024]{1,0:T(8,128)(2,1)S(1)} fusion(bf16[1024,2048]{1,0:T(8,128)(2,1)} %all-gather.5.cloned.1.call-done, f32[1024]{0:T(1024)S(1)} %convert_reduce_fusion, f32[1024]{0:T(1024)S(1)} %add_rsqrt_fusion, bf16[512,1024]{1,0:T(8,128)(2,1)} %copy-done.14, bf16[512,1024]{1,0:T(8,128)(2,1)} %param.17), kind=kOutput, calls=%fused_computation.38 | convolution fusion | flops 2155872256 | bytes 6299648 | tf_op jit(solution)/shard_map/dot_general | solution.py:22
  114.7 5.5 %multiply_reduce_fusion.1 = (f32[1024]{0:T(1024)S(1)}, f32[1024]{0:T(1024)S(1)}, f32[1024,1024]{1,0:T(8,128)S(1)}) fusion(f32[1024]{0:T(1024)S(1)} %convert_element_type.220, f32[1024,1024]{1,0:T(8,128)S(1)} %copy-done.8, bf16[1024,1024]{1,0:T(8,128)(2,1)S(1)} %convolution_convert_fusion.4, bf16[1024,1024]{1,0:T(8,128)(2,1)} %constant_dynamic-update-slice_fusion, ...), kind=kOutput, calls=%fused_computation.15 | convolution fusion | flops 2159015936 | bytes 14692352 | tf_op jit(solution)/shard_map/dot_general | solution.py:22
  124.0 5.2 %fusion.14 = (f32[1024,1024]{1,0:T(8,128)}, bf16[1024,1024]{1,0:T(8,128)(2,1)}, f32[1024]{0:T(1024)S(1)}) fusion(f32[1024]{0:T(1024)S(1)} %bitcast.89, f32[1024,1024]{1,0:T(8,128)S(1)} %get-tuple-element.157, f32[1024]{0:T(1024)S(1)} %bitcast.88, f32[1024]{0:T(1024)S(1)} %bitcast.85, f32[1024]{0:T(1024)S(1)} %convert_element_type.220, ...), kind=kLoop, calls=%fused_computation.34 | loop fusion | flops 22019072 | bytes 16797696 | tf_op jit(solution)/shard_map/mul | solution.py:512
  129.1 33.2 %mix_backward.1 = (bf16[1024,1408]{1,0:T(8,128)(2,1)}, f32[8,1024]{1,0:T(8,128)S(1)}, f32[8,256]{1,0:T(8,128)S(1)}, f32[8,128]{1,0:T(8,128)S(1)}) custom-call(s32[1]{0:T(128)} %bitcast.turn_ref, bf16[1024,1408]{1,0:T(8,128)(2,1)} %convolution_convert_fusion.1.u_ref.s_ref.step_ref, bf16[1024,1408]{1,0:T(8,128)(2,1)} %convolution_convert_fusion.1.u_ref.s_ref.step_ref, ...), custom_call_target="tpu_custom_call" | custom-call | flops 9395240960 | bytes 20971520 | tf_op jit(solution)/shard_map/mix_backward/pallas_call | solution.py:363
  162.4 7.1 %convolution_convert_fusion = bf16[1024,1408]{1,0:T(8,128)(2,1)} fusion(bf16[1024,1408]{1,0:T(8,128)(2,1)} %get-tuple-element.28, f32[1024]{0:T(1024)S(1)} %convert_reduce_fusion, f32[1024]{0:T(1024)S(1)} %add_rsqrt_fusion, bf16[512,1024]{1,0:T(8,128)(2,1)S(1)} %copy-done.15, bf16[512,1024]{1,0:T(8,128)(2,1)S(1)} %copy-done.3), kind=kOutput, calls=%fused_computation.17 | convolution fusion | flops 2961571840 | bytes 7872512 | tf_op jit(solution)/shard_map/dot_general | solution.py:30
  169.6 5.7 %convolution_convert_fusion.3 = bf16[1024,1024]{0,1:T(8,128)(2,1)} fusion(bf16[1024,1024]{1,0:T(8,128)(2,1)} %get-tuple-element.121, f32[1024]{0:T(1024)S(1)} %convert_reduce_fusion, f32[1024]{0:T(1024)S(1)} %add_rsqrt_fusion, bf16[512,1024]{1,0:T(8,128)(2,1)S(1)} %copy-done.16, bf16[512,1024]{1,0:T(8,128)(2,1)S(1)} %copy-done.4), kind=kOutput, calls=%fused_computation.37 | convolution fusion | flops 2155872256 | bytes 6299648 | tf_op jit(solution)/shard_map/dot_general | solution.py:30
  175.2 6.2 %convolution_convert_fusion.2 = bf16[1024,1024]{0,1:T(8,128)(2,1)} fusion(bf16[1024,1024]{1,0:T(8,128)(2,1)} %constant_dynamic-update-slice_fusion, f32[1024]{0:T(1024)S(1)} %bitcast.86, f32[1024]{0:T(1024)S(1)} %convert_element_type.220, f32[1024,1024]{1,0:T(8,128)S(1)} %copy-done.9, bf16[1024,1024]{1,0:T(8,128)(2,1)S(1)} %copy-done.12), kind=kOutput, calls=%fused_computation.36 | convolution fusion | flops 2157969408 | bytes 10493952 | tf_op jit(solution)/shard_map/dot_general | solution.py:30
  181.4 51.8 %reduce-scatter.9.cloned.1.call-done = bf16[64,1408]{1,0:T(8,128)(2,1)} async-done(((bf16[1024,1408]{1,0:T(8,128)(2,1)}), bf16[64,1408]{1,0:T(8,128)(2,1)}) %reduce-scatter.9.cloned.1.call-update) | async-done | bytes 180240
  235.1 4.7 %pad_maximum_fusion = bf16[1024,2048]{0,1:T(8,128)(2,1)} fusion(bf16[1024,1024]{0,1:T(8,128)(2,1)} %convolution_convert_fusion.2, bf16[1024,1024]{0,1:T(8,128)(2,1)} %convolution_convert_fusion.3), kind=kLoop, calls=%fused_computation.10 | loop fusion | flops 8388608 | bytes 8388608 | tf_op jit(solution)/shard_map/concatenate | solution.py:515
  239.8 6.5 %copy.139 = bf16[1024,2048]{1,0:T(8,128)(2,1)} copy(bf16[1024,2048]{0,1:T(8,128)(2,1)} %pad_maximum_fusion) | data formatting | bytes 8388608
  246.5 4.7 %fusion.19 = f32[1024,1024]{1,0:T(8,128)S(1)} fusion(bf16[1024,1024]{1,0:T(8,128)(2,1)} %get-tuple-element.121, bf16[1024,2048]{1,0:T(8,128)(2,1)} %all-gather.5.cloned.1.call-done), kind=kOutput, calls=%fused_computation.43 | convolution fusion | flops 2147483648 | bytes 8388608 | tf_op jit(solution)/shard_map/dot_general | solution.py:26
  252.4 3.4 convolution_add_fusion
  260.3 4.5 %fusion.15 = f32[1024,1024]{1,0:T(8,128)} fusion(bf16[1024,2048]{1,0:T(8,128)(2,1)S(1)} %copy-done.25, f32[1024]{0:T(1024)S(1)} %bitcast.87, f32[1024]{0:T(1024)S(1)} %convert_element_type.220, f32[1024,1024]{1,0:T(8,128)S(1)} %copy-done.10, bf16[1024,1024]{1,0:T(8,128)(2,1)S(1)} %copy-done.13), kind=kOutput, calls=%fused_computation.39 | convolution fusion | flops 2156920832 | bytes 12591104 | tf_op jit(solution)/shard_map/dot_general | solution.py:26
  269.5 4.1 %collective-permute-done.8 = f32[8,1408]{1,0:T(8,128)S(1)} collective-permute-done((f32[8,1408]{1,0:T(8,128)S(1)}, f32[8,1408]{1,0:T(8,128)S(1)}, u32[]{:S(2)}, u32[]{:S(2)}) %collective-permute-start.8) | collective-permute-done | bytes 45088 | tf_op jit(solution)/shard_map/ppermute | solution.py:454
  276.0 7.4 %collective-permute-done.4 = bf16[512,1024]{1,0:T(8,128)(2,1)} collective-permute-done((bf16[512,1024]{1,0:T(8,128)(2,1)}, bf16[512,1024]{1,0:T(8,128)(2,1)}, u32[]{:S(2)}, u32[]{:S(2)}) %collective-permute-start.4) | collective-permute-done | bytes 1048608 | tf_op jit(solution)/shard_map/ppermute | solution.py:441
  286.0 19.0 %collective-permute-done.3 = bf16[512,1024]{1,0:T(8,128)(2,1)} collective-permute-done((bf16[512,1024]{1,0:T(8,128)(2,1)}, bf16[512,1024]{1,0:T(8,128)(2,1)}, u32[]{:S(2)}, u32[]{:S(2)}) %collective-permute-start.3) | collective-permute-done | bytes 1048608 | tf_op jit(solution)/shard_map/ppermute | solution.py:441
  305.0 5.1 %fusion.11 = (f32[512,1024]{1,0:T(8,128)}, bf16[512,1024]{1,0:T(8,128)(2,1)}) fusion(bf16[512,1024]{1,0:T(8,128)(2,1)S(1)} %copy-done.4, bf16[512,1024]{1,0:T(8,128)(2,1)S(1)} %copy-done.7, bf16[512,1024]{1,0:T(8,128)(2,1)} %collective-permute-done.4, f32[1024,1024]{1,0:T(8,128)S(1)} %copy-done.6, f32[512]{0:T(512)S(1)} %broadcast_multiply_fusion, ...), kind=kLoop, calls=%fused_computation.26 | loop fusion | flops 7340032 | bytes 11542528 | tf_op jit(solution)/shard_map/add | solution.py:539
  313.5 19.8 %reduce-scatter.7.cloned.1.call-done = bf16[64,2048]{1,0:T(8,128)(2,1)} async-done(((bf16[1024,2048]{1,0:T(8,128)(2,1)}), bf16[64,2048]{1,0:T(8,128)(2,1)}) %reduce-scatter.7.cloned.1.call-update) | async-done | bytes 262160
  334.8 5.1 %all-reduce.1 = (f32[64]{0:T(128)S(1)}, f32[8,256]{1,0:T(8,128)S(1)}) all-reduce(f32[64]{0:T(128)S(1)} %add_add_fusion, f32[8,256]{1,0:T(8,128)S(1)} %slice-done), channel_id=1, replica_groups=mesh['fsdp'=16,'tp'=2] {'tp'}, use_global_device_ids=true, to_apply=%region_10.11 | all-reduce | flops 2112 | bytes 16896 | tf_op jit(solution)/shard_map/psum | solution.py:554
  (169 shorter events, 60.9 us)
Async XLA Ops:
  7.2 32.4 %copy-start.2 = (bf16[512,1024]{1,0:T(8,128)(2,1)S(1)}, bf16[512,1024]{1,0:T(8,128)(2,1)}, u32[]{:S(2)}) copy-start(bf16[512,1024]{1,0:T(8,128)(2,1)} %param.17) | copy-start | bytes 3145732
  7.2 56.4 %all-gather.3.cloned.1.call-start = ((), (), s32[]{:S(2)}) async-start(), calls=%async_computation.2 | async-start | bytes 3063808 | tf_op jit(solution)/shard_map/all_gather | solution.py:446
  10.6 99.3 %all-gather.5.cloned.1.call-start = ((), (), s32[]{:S(2)}) async-start(), calls=%async_computation.3 | async-start | bytes 4456448 | tf_op jit(solution)/shard_map/all_gather | solution.py:446
  12.3 220.9 %reduce-scatter.9.cloned.1.call-start = ((), (), s32[]{:S(2)}) async-start(), calls=%async_computation.6 | async-start | bytes 3063808
  12.4 27.2 %collective-permute-start = (bf16[512,1024]{1,0:T(8,128)(2,1)}, bf16[512,1024]{1,0:T(8,128)(2,1)S(1)}, u32[]{:S(2)}, u32[]{:S(2)}) collective-permute-start(bf16[512,1024]{1,0:T(8,128)(2,1)} %param.17), channel_id=1, source_target_pairs={{0,1},{1,0},{2,3},{3,2},{4,5},{5,4},{6,7},{7,6},{8,9},{9,8},{10,11... | collective-permute-start | bytes 3145736 | tf_op jit(solution)/shard_map/ppermute | solution.py:436
  15.4 45.9 %collective-permute-start.1 = (bf16[512,1024]{1,0:T(8,128)(2,1)}, bf16[512,1024]{1,0:T(8,128)(2,1)}, u32[]{:S(2)}, u32[]{:S(2)}) collective-permute-start(bf16[512,1024]{1,0:T(8,128)(2,1)} %param.33), channel_id=1, source_target_pairs={{0,1},{1,0},{2,3},{3,2},{4,5},{5,4},{6,7},{7,6},{8,9},{9,8},{10,11... | collective-permute-start | bytes 3145736 | tf_op jit(solution)/shard_map/ppermute | solution.py:436
  39.6 33.2 %copy-start.14 = (bf16[512,1024]{1,0:T(8,128)(2,1)}, bf16[512,1024]{1,0:T(8,128)(2,1)S(1)}, u32[]{:S(2)}) copy-start(bf16[512,1024]{1,0:T(8,128)(2,1)S(1)} %collective-permute-done) | copy-start | bytes 3145732
  120.2 3.7 %collective-permute-start.2 = (f32[1024,2]{0,1:T(2,128)S(1)}, f32[1024,2]{0,1:T(2,128)S(1)}, u32[]{:S(2)}, u32[]{:S(2)}) collective-permute-start(f32[1024,2]{0,1:T(2,128)S(1)} %pad_maximum_fusion.5), channel_id=1, source_target_pairs={{0,1},{1,0},{2,3},{3,2},{4,5},{5,4},{6,7},{7,6},{8,9},{9,8},{10,11... | collective-permute-start | bytes 24584 | tf_op jit(solution)/shard_map/ppermute | solution.py:504
  129.1 33.2 %copy-start.3 = (bf16[512,1024]{1,0:T(8,128)(2,1)S(1)}, bf16[512,1024]{1,0:T(8,128)(2,1)}, u32[]{:S(2)}) copy-start(bf16[512,1024]{1,0:T(8,128)(2,1)} %param.17) | copy-start | bytes 3145732
  129.1 33.2 %copy-start.15 = (bf16[512,1024]{1,0:T(8,128)(2,1)S(1)}, bf16[512,1024]{1,0:T(8,128)(2,1)}, u32[]{:S(2)}) copy-start(bf16[512,1024]{1,0:T(8,128)(2,1)} %copy-done.14) | copy-start | bytes 3145732
  169.5 142.4 %all-reduce.4.cloned.1.call-start = ((), (), s32[]{:S(2)}) async-start(), calls=%async_computation.4 | async-start | bytes 262144 | tf_op jit(solution)/shard_map/psum | solution.py:554
  235.1 98.2 %reduce-scatter.7.cloned.1.call-start = ((), (), s32[]{:S(2)}) async-start(), calls=%async_computation.5 | async-start | bytes 4456448
  246.4 4.8 %collective-permute-start.5 = (f32[8,1408]{1,0:T(8,128)S(1)}, f32[8,1408]{1,0:T(8,128)S(1)}, u32[]{:S(2)}, u32[]{:S(2)}) collective-permute-start(f32[8,1408]{1,0:T(8,128)S(1)} %pad_maximum_fusion.3), channel_id=1, source_target_pairs={{0,2},{2,0},{4,6},{6,4},{8,10},{10,8},{12,14},{14,12},{16,18},{18,... | collective-permute-start | bytes 135176 | tf_op jit(solution)/shard_map/ppermute | solution.py:454
  251.3 7.2 %collective-permute-start.6 = (f32[8,1408]{1,0:T(8,128)S(1)}, f32[8,1408]{1,0:T(8,128)S(1)}, u32[]{:S(2)}, u32[]{:S(2)}) collective-permute-start(f32[8,1408]{1,0:T(8,128)S(1)} %fusion.46), channel_id=1, source_target_pairs={{0,4},{2,6},{4,0},{6,2},{8,12},{10,14},{12,8},{14,10},{16,20},{18,... | collective-permute-start | bytes 135176 | tf_op jit(solution)/shard_map/ppermute | solution.py:454
  257.1 26.3 %collective-permute-start.4 = (bf16[512,1024]{1,0:T(8,128)(2,1)}, bf16[512,1024]{1,0:T(8,128)(2,1)}, u32[]{:S(2)}, u32[]{:S(2)}) collective-permute-start(bf16[512,1024]{1,0:T(8,128)(2,1)} %slice.286), channel_id=1, source_target_pairs={{0,1},{1,0},{2,3},{3,2},{4,5},{5,4},{6,7},{7,6},{8,9},{9,8},{10,11... | collective-permute-start | bytes 3145736 | tf_op jit(solution)/shard_map/ppermute | solution.py:441
  258.6 9.5 %collective-permute-start.7 = (f32[8,1408]{1,0:T(8,128)S(1)}, f32[8,1408]{1,0:T(8,128)S(1)}, u32[]{:S(2)}, u32[]{:S(2)}) collective-permute-start(f32[8,1408]{1,0:T(8,128)S(1)} %add.87), channel_id=1, source_target_pairs={{0,8},{2,10},{4,12},{6,14},{8,0},{10,2},{12,4},{14,6},{16,24},{18,... | collective-permute-start | bytes 135176 | tf_op jit(solution)/shard_map/ppermute | solution.py:454
  264.8 40.2 %copy-start.7 = (bf16[512,1024]{1,0:T(8,128)(2,1)S(1)}, bf16[512,1024]{1,0:T(8,128)(2,1)}, u32[]{:S(2)}) copy-start(bf16[512,1024]{1,0:T(8,128)(2,1)} %param.33) | copy-start | bytes 3145732
  267.8 37.2 %collective-permute-start.3 = (bf16[512,1024]{1,0:T(8,128)(2,1)}, bf16[512,1024]{1,0:T(8,128)(2,1)}, u32[]{:S(2)}, u32[]{:S(2)}) collective-permute-start(bf16[512,1024]{1,0:T(8,128)(2,1)} %slice.287), channel_id=1, source_target_pairs={{0,1},{1,0},{2,3},{3,2},{4,5},{5,4},{6,7},{7,6},{8,9},{9,8},{10,11... | collective-permute-start | bytes 3145736 | tf_op jit(solution)/shard_map/ppermute | solution.py:441
  268.1 5.4 %collective-permute-start.8 = (f32[8,1408]{1,0:T(8,128)S(1)}, f32[8,1408]{1,0:T(8,128)S(1)}, u32[]{:S(2)}, u32[]{:S(2)}) collective-permute-start(f32[8,1408]{1,0:T(8,128)S(1)} %add.88), channel_id=1, source_target_pairs={{0,16},{2,18},{4,20},{6,22},{8,24},{10,26},{12,28},{14,30},{16,0},... | collective-permute-start | bytes 135176 | tf_op jit(solution)/shard_map/ppermute | solution.py:454
  273.6 36.5 %copy-start.19 = (f32[8,1408]{1,0:T(8,128)}, f32[8,1408]{1,0:T(8,128)S(1)}, u32[]{:S(2)}) copy-start(f32[8,1408]{1,0:T(8,128)S(1)} %add.89) | copy-start | bytes 135172
  275.5 29.5 %copy-start.6 = (f32[1024,1024]{1,0:T(8,128)S(1)}, f32[1024,1024]{1,0:T(8,128)}, u32[]{:S(2)}) copy-start(f32[1024,1024]{1,0:T(8,128)} %copy-done.5) | copy-start | bytes 12582916
  286.0 25.3 %copy-start.22 = (bf16[64,16]{0,1:T(8,128)(2,1)S(1)}, bf16[64,16]{0,1:T(8,128)(2,1)}, u32[]{:S(2)}) copy-start(bf16[64,16]{0,1:T(8,128)(2,1)} %param.22) | copy-start | bytes 6148
  310.1 24.7 %slice-start = ((f32[8,1408]{1,0:T(8,128)}), f32[8,256]{1,0:T(8,128)S(1)}, s32[]{:S(2)}) async-start(f32[8,1408]{1,0:T(8,128)} %copy-done.19), calls=%async_computation.7 | async-start | bytes 16384 | tf_op jit(solution)/shard_map/slice | solution.py:553
  310.1 31.0 %copy-start.23 = (bf16[64]{0:T(256)(128)(2,1)S(1)}, bf16[64]{0:T(256)(128)(2,1)}, u32[]{:S(2)}) copy-start(bf16[64]{0:T(256)(128)(2,1)} %param.18) | copy-start | bytes 388
  (18 other events, 130.3 us)
Sparse Core Ops, SparseCore 0:
  10.9 46.8 all-gather.2
  60.5 49.3 all-gather.4
  169.6 63.6 reduce-scatter.8
  236.0 20.3 all-reduce.3
  260.6 72.6 reduce-scatter.6
